TPU v7x, 32 devices: a whole 2x2x4 slice. The times are simulated.
32 devices in a mesh: plane: 2 (over core), row: 4 (over z), col: 4 (over y, x).
Axes of the slice: x: 2, y: 2, z: 4, core: 2. Of those that a mesh axis runs over, the one named last changes fastest.
Arguments:
- velocity: float32 [3, 4, 4096, 4096], P(None, 'plane', 'row', 'col'), may hold values from -60 to 60
Outputs:
- dissipation: float32 [4, 4096, 4096], P('plane', 'row', 'col')
- fine_means: float32 [128, 128], P('row', 'col')
- coarse_means: float32 [4, 4], replicated
All inputs are finite; a program needn't handle non-finite values.
Results may differ from a plain program's by a relative error of at most 0.000078.
Values sent between devices are 32-bit elements; how exact they have to be, the bound alone decides.
A program may use at most 320 MiB of HBM per device.

v0:
```python
import math

import jax
import jax.numpy as jnp
from jax import lax
from jax.sharding import PartitionSpec as P

N = 4096
FIRST = 32
FINE = 32
COARSE = 1024


precise = lax.Precision.HIGHEST


def with_halo(cells, sides, width):
    for axis, dim in sides:
        count = lax.axis_size(axis)
        head = lax.slice_in_dim(cells, 0, width, axis=dim)
        tail = lax.slice_in_dim(cells, cells.shape[dim] - width, cells.shape[dim], axis=dim)
        cells = jnp.concatenate(
            [
                lax.ppermute(tail, axis, [(i, (i + 1) % count) for i in range(count)]),
                cells,
                lax.ppermute(head, axis, [((i + 1) % count, i) for i in range(count)]),
            ],
            axis=dim,
        )
    return cells


def angle_table(height, across, modulus):
    left_idx = lax.broadcasted_iota(jnp.int32, (height, across), 0)
    right_idx = lax.broadcasted_iota(jnp.int32, (height, across), 1)
    turn_count = left_idx * right_idx % modulus
    phase_ang = turn_count.astype(jnp.float32) * (2.0 * math.pi / modulus)
    return (jnp.cos(phase_ang), jnp.sin(phase_ang))


def wave_table(first_len, second, length):
    low_idx = lax.broadcasted_iota(jnp.int32, (first_len, second), 0)
    high_idx = lax.broadcasted_iota(jnp.int32, (first_len, second), 1)
    indices = low_idx + first_len * high_idx
    signed = jnp.where(indices < length // 2, indices, indices - length)
    signed = jnp.where(indices == length // 2, 0, signed)
    return signed.astype(jnp.float32) * (2.0 * math.pi / length)


def left_mult(coeffs, values):
    return jnp.einsum("kn,...nm->...km", coeffs, values, precision=precise)


def right_mult(values, coeffs):
    return jnp.einsum("...kn,nm->...km", values, coeffs, precision=precise)


def derivative_last(values):
    length = values.shape[-1]
    first_len = FIRST
    second = length // first_len
    leading = values.shape[:-1]
    blocks = values.reshape(leading + (first_len, second))
    cos_a, sin_a = angle_table(first_len, first_len, first_len)
    cos_b, sin_b = angle_table(second, second, second)
    cos_t, sin_t = angle_table(first_len, second, length)
    forward_a = jnp.concatenate([cos_a, -sin_a], axis=0)
    section_a = left_mult(forward_a, blocks)
    real_a = section_a[..., :first_len, :]
    imag_a = section_a[..., first_len:, :]
    real_b = real_a * cos_t + imag_a * sin_t
    imag_b = imag_a * cos_t - real_a * sin_t
    forward_b = jnp.concatenate(
        [jnp.concatenate([cos_b, -sin_b], axis=1), jnp.concatenate([sin_b, cos_b], axis=1)], axis=0
    )
    section_c = right_mult(jnp.concatenate([real_b, imag_b], axis=-1), forward_b)
    wavenum = wave_table(first_len, second, length)
    scaled = jnp.concatenate(
        [-wavenum * section_c[..., second:], wavenum * section_c[..., :second]], axis=-1
    )
    inverse_b = jnp.concatenate(
        [jnp.concatenate([cos_b, sin_b], axis=1), jnp.concatenate([-sin_b, cos_b], axis=1)], axis=0
    )
    section_e = right_mult(scaled, inverse_b)
    real_e = section_e[..., :second]
    imag_e = section_e[..., second:]
    real_f = real_e * cos_t - imag_e * sin_t
    imag_f = real_e * sin_t + imag_e * cos_t
    inverse_a = jnp.concatenate([cos_a, -sin_a], axis=1)
    result = left_mult(inverse_a, jnp.concatenate([real_f, imag_f], axis=-2)) * (1.0 / length)
    return result.reshape(leading + (length,))


def along_rows(pencil):
    turned = jnp.swapaxes(pencil, 2, 3)
    back_turned = jnp.swapaxes(derivative_last(turned), 2, 3)
    return lax.all_to_all(back_turned, "row", split_axis=2, concat_axis=3, tiled=True)


def along_cols(pencil):
    return lax.all_to_all(derivative_last(pencil), "col", split_axis=3, concat_axis=2, tiled=True)


def per_device(velocity):
    x_local = velocity.shape[2]
    y_local = velocity.shape[3]
    plane_count = velocity.shape[1] * lax.axis_size("plane")
    grad_x = along_rows(lax.all_to_all(velocity, "row", split_axis=3, concat_axis=2, tiled=True))
    grad_y = along_cols(lax.all_to_all(velocity, "col", split_axis=2, concat_axis=3, tiled=True))
    padded = with_halo(velocity, (("plane", 1),), 1)
    grad_z = (padded[:, 2:] - padded[:, :-2]) * 0.5
    cross_xy = grad_y[0] + grad_x[1]
    cross_xz = grad_z[0] + grad_x[2]
    cross_yz = grad_z[1] + grad_y[2]
    dissip = grad_x[0] * grad_x[0] + grad_y[1] * grad_y[1] + grad_z[2] * grad_z[2]
    dissip = dissip + 0.5 * (cross_xy * cross_xy + cross_xz * cross_xz + cross_yz * cross_yz)
    column_sum = jnp.sum(dissip, axis=0)
    fine_local = column_sum.reshape(x_local // FINE, FINE, y_local // FINE, FINE).sum(axis=(1, 3))
    fine_total = lax.psum(fine_local, "plane")
    fine_means = fine_total * (1.0 / (plane_count * FINE * FINE))
    local_total = jnp.sum(fine_total)
    box_count = N // COARSE
    box_row = lax.axis_index("row") * x_local // COARSE
    box_col = lax.axis_index("col") * y_local // COARSE
    rows_hit = (lax.iota(jnp.int32, box_count) == box_row).astype(jnp.float32)
    cols_hit = (lax.iota(jnp.int32, box_count) == box_col).astype(jnp.float32)
    partial_map = rows_hit[:, None] * cols_hit[None, :] * local_total
    coarse_total = lax.psum(partial_map, ("row", "col"))
    coarse_means = coarse_total * (1.0 / (plane_count * COARSE * COARSE))
    return (dissip, fine_means, coarse_means)


def solution(mesh):
    in_specs = (P(None, "plane", "row", "col"),)
    out_specs = (P("plane", "row", "col"), P("row", "col"), P())
    return jax.shard_map(
        per_device, mesh=mesh, in_specs=in_specs, out_specs=out_specs, check_vma=False
    )
```

profile of v0, /device:TPU:0, one launch (start us, length us, event | category | flops | bytes accessed | tf_op | source)
XLA Modules:
  0.0 3044.5 jit_solution(17018088844829984537)
XLA Ops:
  0.6 33.4 %copy.212 = f32[3,2,1024,1024]{3,0,1,2:T(4,128)} copy(f32[3,2,1024,1024]{3,2,1,0:T(8,128)} %param.1) | data formatting | bytes 50331648 | tf_op args[0]
  34.1 9.8 all-to-all-start.2
  43.9 36.0 %copy.201 = f32[3,2,1024,1024]{2,0,1,3:T(4,128)} copy(f32[3,2,1024,1024]{3,2,1,0:T(8,128)} %param.1) | data formatting | bytes 50331648 | tf_op args[0]
  79.9 327.5 %all-to-all-done.2 = f32[3,2,1024,1024]{3,0,1,2:T(4,128)} async-done(((f32[3,2,1024,1024]{3,0,1,2:T(4,128)}), f32[3,2,1024,1024]{3,0,1,2:T(4,128)}, u32[]{:S(2)}, u32[]{:S(2)}) %all-to-all-start.2) | async-done | bytes 25165856 | tf_op jit(solution)/shard_map/all_to_all | solution.py:109
  407.3 9.9 all-to-all-start
  420.2 31.7 %copy.290 = f32[3,2,4,256,1024]{4,2,3,1,0:T(4,128)} copy(f32[3,2,4,256,1024]{4,0,1,3,2:T(4,128)} %bitcast.17) | data formatting | bytes 50331648 | tf_op jit(solution)/shard_map/all_to_all | solution.py:109
  451.8 29.5 reshape.167
  481.4 46.3 %convolution_bitcast_fusion = f32[3,2,256,64,128]{4,3,2,1,0:T(8,128)} fusion(f32[3,2,256,32,128]{4,3,2,1,0:T(8,128)} %reshape.167, f32[32,32]{0,1:T(8,128)S(1)} %get-tuple-element.49, f32[32,32]{0,1:T(8,128)S(1)} %get-tuple-element.50), kind=kOutput, calls=%fused_computation.35 | convolution fusion | flops 4831840256 | bytes 75505664 | tf_op jit(solution)/shard_map/kn,...nm->...km/dot_general | solution.py:51
  527.6 611.7 %all-to-all-done = f32[3,2,1024,1024]{2,0,1,3:T(4,128)} async-done(((f32[3,2,1024,1024]{2,0,1,3:T(4,128)}), f32[3,2,1024,1024]{2,0,1,3:T(4,128)}, u32[]{:S(2)}, u32[]{:S(2)}) %all-to-all-start) | async-done | bytes 25165856 | tf_op jit(solution)/shard_map/all_to_all | solution.py:108
  1139.4 32.1 %copy.202 = f32[3,2,4,1024,256]{3,2,4,1,0:T(4,128)} copy(f32[3,2,4,1024,256]{3,0,1,4,2:T(4,128)} %bitcast.3) | data formatting | bytes 50331648 | tf_op jit(solution)/shard_map/all_to_all | solution.py:108
  1171.5 30.2 all_to_all.49
  1201.6 13.3 copy.261
  1215.0 44.2 %convolution_bitcast_fusion.1 = f32[3,2,256,64,128]{4,3,2,1,0:T(8,128)} fusion(f32[3,2,256,32,128]{4,3,2,1,0:T(8,128)S(1)} %bitcast.104, f32[32,32]{0,1:T(8,128)S(1)} %get-tuple-element.49, f32[32,32]{0,1:T(8,128)S(1)} %get-tuple-element.50), kind=kOutput, calls=%fused_computation.36 | convolution fusion | flops 4831840256 | bytes 75505664 | tf_op jit(solution)/shard_map/kn,...nm->...km/dot_general | solution.py:51
  1259.2 67.7 %multiply_add_fusion.3 = (f32[3,2,256,32,128]{4,3,2,1,0:T(8,128)}, f32[3,2,256,32,128]{4,3,2,1,0:T(8,128)}, f32[3,2,256,32,128]{4,3,2,1,0:T(8,128)}, f32[3,2,256,32,128]{4,3,2,1,0:T(8,128)}) fusion(f32[3,2,256,64,128]{4,3,2,1,0:T(8,128)} %convolution_bitcast_fusion.1, f32[32,128]{1,0:T(8,128)S(1)} %get-tuple-element.51, f32[32,128]{1,0:T(8,128)S(1)} %get-tuple-element.52, ...), kind=kLoop, calls=%fused_computation.34 | loop fusion | flops 75497472 | bytes 201359360 | tf_op jit(solution)/shard_map/add | solution.py:71
  1326.9 34.6 %pad_maximum_fusion = f32[3,2,256,32,256]{4,3,2,1,0:T(8,128)} fusion(f32[3,2,256,32,128]{4,3,2,1,0:T(8,128)} %get-tuple-element.18, f32[3,2,256,32,128]{4,3,2,1,0:T(8,128)} %get-tuple-element.17), kind=kLoop, calls=%fused_computation | loop fusion | flops 12582912 | bytes 100663296 | tf_op jit(solution)/shard_map/concatenate | solution.py:76
  1361.5 84.8 %fusion.10 = f32[3,2,256,32,256]{2,4,3,1,0:T(8,128)} fusion(f32[3,2,256,32,256]{4,3,2,1,0:T(8,128)} %pad_maximum_fusion, f32[128,128]{0,1:T(8,128)S(1)} %copy-done.5, f32[128,128]{0,1:T(8,128)S(1)} %copy-done.3, f32[128,128]{0,1:T(8,128)S(1)} %copy-done.1), kind=kOutput, calls=%fused_computation.14 | convolution fusion | flops 38654902272 | bytes 100859904 | tf_op jit(solution)/shard_map/...kn,nm->...km/dot_general | solution.py:55
  1446.2 34.4 %pad_maximum_fusion.2 = f32[3,2,256,32,256]{4,3,2,1,0:T(8,128)} fusion(f32[3,2,256,32,128]{4,3,2,1,0:T(8,128)} %get-tuple-element.43, f32[3,2,256,32,128]{4,3,2,1,0:T(8,128)} %get-tuple-element.44), kind=kLoop, calls=%fused_computation.6 | loop fusion | flops 12582912 | bytes 100663296 | tf_op jit(solution)/shard_map/concatenate | solution.py:76
  1480.7 85.2 %fusion.8 = f32[3,2,256,32,256]{2,4,3,1,0:T(8,128)} fusion(f32[3,2,256,32,256]{4,3,2,1,0:T(8,128)} %pad_maximum_fusion.2, f32[128,128]{0,1:T(8,128)S(1)} %copy-done.5, f32[128,128]{0,1:T(8,128)S(1)} %copy-done.3, f32[128,128]{0,1:T(8,128)S(1)} %copy-done.1), kind=kOutput, calls=%fused_computation.12 | convolution fusion | flops 38654902272 | bytes 100859904 | tf_op jit(solution)/shard_map/...kn,nm->...km/dot_general | solution.py:55
  1565.9 63.6 %slice_multiply_fusion.1 = (f32[3,2,256,32,128]{2,4,3,1,0:T(8,128)}, f32[3,2,256,32,128]{2,4,3,1,0:T(8,128)}, f32[3,2,256,32,128]{2,4,3,1,0:T(8,128)}, f32[3,2,256,32,128]{2,4,3,1,0:T(8,128)}) fusion(f32[3,2,256,32,256]{2,4,3,1,0:T(8,128)} %fusion.8, f32[32,128]{1,0:T(8,128)S(1)} %copy-done.16, f32[32,128]{1,0:T(8,128)S(1)} %copy-done.17, ...), kind=kLoop, calls=%fused_computation.21 | loop fusion | flops 25165824 | bytes 201359360 | tf_op jit(solution)/shard_map/mul | solution.py:79
  1629.5 34.3 %pad_maximum_fusion.3 = f32[3,2,256,32,256]{2,4,3,1,0:T(8,128)} fusion(f32[3,2,256,32,128]{2,4,3,1,0:T(8,128)} %get-tuple-element.26, f32[3,2,256,32,128]{2,4,3,1,0:T(8,128)} %get-tuple-element.25), kind=kLoop, calls=%fused_computation.7 | loop fusion | flops 12582912 | bytes 100663296 | tf_op jit(solution)/shard_map/concatenate | solution.py:78
  1663.8 49.7 %copy.246 = f32[3,2,256,32,256]{4,3,2,1,0:T(8,128)} copy(f32[3,2,256,32,256]{2,4,3,1,0:T(8,128)} %pad_maximum_fusion.3) | data formatting | bytes 100663296 | tf_op jit(solution)/shard_map/concatenate | solution.py:78
  1713.5 34.3 %pad_maximum_fusion.1 = f32[3,2,256,32,256]{2,4,3,1,0:T(8,128)} fusion(f32[3,2,256,32,128]{2,4,3,1,0:T(8,128)} %get-tuple-element.39, f32[3,2,256,32,128]{2,4,3,1,0:T(8,128)} %get-tuple-element.40), kind=kLoop, calls=%fused_computation.1 | loop fusion | flops 12582912 | bytes 100663296 | tf_op jit(solution)/shard_map/concatenate | solution.py:78
  1747.8 49.7 %copy.242 = f32[3,2,256,32,256]{4,3,2,1,0:T(8,128)} copy(f32[3,2,256,32,256]{2,4,3,1,0:T(8,128)} %pad_maximum_fusion.1) | data formatting | bytes 100663296 | tf_op jit(solution)/shard_map/concatenate | solution.py:78
  1797.5 47.2 %fusion.36 = f32[3,2,256,32,256]{4,3,2,1,0:T(8,128)} fusion(f32[3,2,256,32,256]{4,3,2,1,0:T(8,128)} %copy.246, f32[256,256,1,1,1]{0,1,4,3,2:T(8,128)S(1)} %copy-done.7), kind=kOutput, calls=%fused_computation.68 | convolution fusion | flops 38654705664 | bytes 100925440 | tf_op jit(solution)/shard_map/...kn,nm->...km/dot_general | solution.py:55
  1844.7 47.2 %fusion.38 = f32[3,2,256,32,256]{4,3,2,1,0:T(8,128)} fusion(f32[3,2,256,32,256]{4,3,2,1,0:T(8,128)} %copy.242, f32[256,256,1,1,1]{0,1,4,3,2:T(8,128)S(1)} %copy-done.6), kind=kOutput, calls=%fused_computation.69 | convolution fusion | flops 38654705664 | bytes 100925440 | tf_op jit(solution)/shard_map/...kn,nm->...km/dot_general | solution.py:55
  1891.9 68.2 %multiply_subtract_fusion.2 = (f32[3,2,256,32,128]{4,3,2,1,0:T(8,128)}, f32[3,2,256,32,128]{4,3,2,1,0:T(8,128)}, f32[3,2,256,32,128]{4,3,2,1,0:T(8,128)}, f32[3,2,256,32,128]{4,3,2,1,0:T(8,128)}) fusion(f32[3,2,256,32,256]{4,3,2,1,0:T(8,128)} %fusion.38, f32[32,128]{1,0:T(8,128)S(1)} %copy-done.13, f32[32,128]{1,0:T(8,128)S(1)} %copy-done.15, ...), kind=kLoop, calls=%fused_computation.32 | loop fusion | flops 75497472 | bytes 201359360 | tf_op jit(solution)/shard_map/sub | solution.py:87
  1960.1 34.9 %multiply_bitcast_fusion = f32[3,2,256,32,128]{4,3,2,1,0:T(8,128)} fusion(f32[3,2,256,32,128]{4,3,2,1,0:T(8,128)} %get-tuple-element.41, f32[3,2,256,32,128]{4,3,2,1,0:T(8,128)} %get-tuple-element.42, f32[32,32]{0,1:T(8,128)S(1)} %copy-done.9, f32[32,32]{0,1:T(8,128)S(1)} %copy-done.11), kind=kOutput, calls=%fused_computation.25 | convolution fusion | flops 4850714624 | bytes 75505664 | tf_op jit(solution)/shard_map/kn,...nm->...km/dot_general | solution.py:51
  1995.0 29.3 copy.257
  2032.8 34.9 %multiply_bitcast_fusion.1 = f32[3,2,256,32,128]{4,3,2,1,0:T(8,128)} fusion(f32[3,2,256,32,128]{4,3,2,1,0:T(8,128)} %get-tuple-element.16, f32[3,2,256,32,128]{4,3,2,1,0:T(8,128)} %get-tuple-element.15, f32[32,32]{0,1:T(8,128)S(1)} %copy-done.9, f32[32,32]{0,1:T(8,128)S(1)} %copy-done.11), kind=kOutput, calls=%fused_computation.30 | convolution fusion | flops 4850714624 | bytes 75505664 | tf_op jit(solution)/shard_map/kn,...nm->...km/dot_general | solution.py:51
  2067.7 29.2 copy.253
  2096.9 207.4 %all-to-all-done.3 = f32[3,2,256,4096]{2,1,0,3:T(2,128)} async-done(((f32[3,2,256,4096]{2,1,0,3:T(2,128)}), f32[3,2,256,4096]{2,1,0,3:T(2,128)}, u32[]{:S(2)}, u32[]{:S(2)}) %all-to-all-start.3) | async-done | bytes 25165856 | tf_op jit(solution)/shard_map/all_to_all | solution.py:101
  2312.8 25.1 copy.224
  2338.0 19.3 fusion.80
  2358.3 18.4 collective-permute-done
  2376.7 18.0 collective-permute-done.1
  2394.7 25.4 fusion.13
  2420.1 18.1 fusion.79
  2464.3 36.9 %copy.221 = f32[3,2,256,4,1024]{4,2,3,1,0:T(8,128)} copy(f32[3,2,256,4,1024]{2,1,0,4,3:T(2,128)} %bitcast.25) | data formatting | bytes 50331648 | tf_op jit(solution)/shard_map/all_to_all | solution.py:101
  2501.2 18.2 slice_multiply_fusion.5
  2519.4 10.5 mul.501
  2529.9 10.6 squeeze.38
  2540.5 10.6 squeeze.41
  2577.2 277.7 %all-to-all-done.1 = f32[3,2,4096,256]{3,1,0,2:T(2,128)} async-done(((f32[3,2,4096,256]{3,1,0,2:T(2,128)}), f32[3,2,4096,256]{3,1,0,2:T(2,128)}, u32[]{:S(2)}, u32[]{:S(2)}) %all-to-all-start.1) | async-done | bytes 25165856 | tf_op jit(solution)/shard_map/all_to_all | solution.py:97
  2854.9 19.0 copy.210
  2873.9 37.5 %fusion.28 = (f32[1024,4,256]{2,0,1:T(8,128)}, f32[1,2,1024,4,256]{4,2,3,1,0:T(8,128)}, f32[1,2,1024,4,256]{4,2,3,1,0:T(8,128)}, f32[1,2,1024,4,256]{4,2,3,1,0:T(8,128)}) fusion(f32[1,2,1024,4,256]{4,2,3,1,0:T(8,128)} %copy.235, f32[1,2,1024,4,256]{4,3,2,1,0:T(4,128)} %squeeze.41, f32[1,2,1024,4,256]{4,3,2,1,0:T(4,128)} %squeeze.38, ...), kind=kLoop, calls=%fused_computation.54 | loop fusion | flops 28311552 | bytes 104857600 | tf_op jit(solution)/shard_map/reduce_sum | solution.py:117
  2937.6 29.8 fusion.21
  2981.5 11.6 reshape.169
  3005.0 37.9 %psum.15 = f32[4,4]{1,0:T(4,128)S(1)} all-reduce(f32[4,4]{1,0:T(4,128)S(1)} %multiply_multiply_fusion), channel_id=1, replica_groups=mesh['plane'=2,'row'=4,'col'=4] {'row','col'}, use_global_device_ids=true, to_apply=%region_4.5 | all-reduce | flops 16 | bytes 128 | tf_op jit(solution)/shard_map/psum | solution.py:128
  (70 shorter events, 126.6 us)
Async XLA Ops:
  34.1 373.3 %all-to-all-start.2 = ((f32[3,2,1024,1024]{3,0,1,2:T(4,128)}), f32[3,2,1024,1024]{3,0,1,2:T(4,128)}, u32[]{:S(2)}, u32[]{:S(2)}) async-start(f32[3,2,1024,1024]{3,0,1,2:T(4,128)} %copy.212), calls=%async_computation.2 | async-start | bytes 67108864 | tf_op jit(solution)/shard_map/all_to_all | solution.py:109
  407.3 732.1 %all-to-all-start = ((f32[3,2,1024,1024]{2,0,1,3:T(4,128)}), f32[3,2,1024,1024]{2,0,1,3:T(4,128)}, u32[]{:S(2)}, u32[]{:S(2)}) async-start(f32[3,2,1024,1024]{2,0,1,3:T(4,128)} %copy.201), calls=%async_computation | async-start | bytes 67108864 | tf_op jit(solution)/shard_map/all_to_all | solution.py:108
  417.4 797.6 %copy-start.8 = (f32[32,32]{0,1:T(8,128)}, f32[32,32]{0,1:T(8,128)S(1)}, u32[]{:S(2)}) copy-start(f32[32,32]{0,1:T(8,128)S(1)} %get-tuple-element.49) | copy-start | bytes 12292
  417.4 797.6 %copy-start.10 = (f32[32,32]{0,1:T(8,128)}, f32[32,32]{0,1:T(8,128)S(1)}, u32[]{:S(2)}) copy-start(f32[32,32]{0,1:T(8,128)S(1)} %get-tuple-element.50) | copy-start | bytes 12292
  417.5 841.7 %copy-start.12 = (f32[32,128]{1,0:T(8,128)}, f32[32,128]{1,0:T(8,128)S(1)}, u32[]{:S(2)}) copy-start(f32[32,128]{1,0:T(8,128)S(1)} %get-tuple-element.51) | copy-start | bytes 49156
  417.5 841.7 %copy-start.14 = (f32[32,128]{1,0:T(8,128)}, f32[32,128]{1,0:T(8,128)S(1)}, u32[]{:S(2)}) copy-start(f32[32,128]{1,0:T(8,128)S(1)} %get-tuple-element.52) | copy-start | bytes 49156
  417.8 1.0 copy-start
  418.1 1.5 copy-start.2
  418.1 2.1 copy-start.4
  1326.9 34.6 %copy-start.1 = (f32[128,128]{0,1:T(8,128)S(1)}, f32[128,128]{0,1:T(8,128)}, u32[]{:S(2)}) copy-start(f32[128,128]{0,1:T(8,128)} %copy-done) | copy-start | bytes 196612
  1326.9 34.6 %copy-start.3 = (f32[128,128]{0,1:T(8,128)S(1)}, f32[128,128]{0,1:T(8,128)}, u32[]{:S(2)}) copy-start(f32[128,128]{0,1:T(8,128)} %copy-done.2) | copy-start | bytes 196612
  1326.9 34.6 %copy-start.5 = (f32[128,128]{0,1:T(8,128)S(1)}, f32[128,128]{0,1:T(8,128)}, u32[]{:S(2)}) copy-start(f32[128,128]{0,1:T(8,128)} %copy-done.4) | copy-start | bytes 196612
  1480.7 85.2 %copy-start.16 = (f32[32,128]{1,0:T(8,128)S(1)}, f32[32,128]{1,0:T(8,128)}, u32[]{:S(2)}) copy-start(f32[32,128]{1,0:T(8,128)} %get-tuple-element.47) | copy-start | bytes 49156
  1480.7 85.2 %copy-start.17 = (f32[32,128]{1,0:T(8,128)S(1)}, f32[32,128]{1,0:T(8,128)}, u32[]{:S(2)}) copy-start(f32[32,128]{1,0:T(8,128)} %get-tuple-element.48) | copy-start | bytes 49156
  1747.8 49.7 %copy-start.7 = (f32[256,256,1,1,1]{0,1,4,3,2:T(8,128)S(1)}, f32[256,256,1,1,1]{0,1,4,3,2:T(8,128)}, u32[]{:S(2)}) copy-start(f32[256,256,1,1,1]{0,1,4,3,2:T(8,128)} %fusion.89) | copy-start | bytes 786436
  1797.5 47.2 %copy-start.6 = (f32[256,256,1,1,1]{0,1,4,3,2:T(8,128)S(1)}, f32[256,256,1,1,1]{0,1,4,3,2:T(8,128)}, u32[]{:S(2)}) copy-start(f32[256,256,1,1,1]{0,1,4,3,2:T(8,128)} %fusion.91) | copy-start | bytes 786436
  1844.6 47.2 %copy-start.13 = (f32[32,128]{1,0:T(8,128)S(1)}, f32[32,128]{1,0:T(8,128)}, u32[]{:S(2)}) copy-start(f32[32,128]{1,0:T(8,128)} %copy-done.12) | copy-start | bytes 49156
  1844.6 47.2 %copy-start.15 = (f32[32,128]{1,0:T(8,128)S(1)}, f32[32,128]{1,0:T(8,128)}, u32[]{:S(2)}) copy-start(f32[32,128]{1,0:T(8,128)} %copy-done.14) | copy-start | bytes 49156
  1891.8 68.2 %copy-start.9 = (f32[32,32]{0,1:T(8,128)S(1)}, f32[32,32]{0,1:T(8,128)}, u32[]{:S(2)}) copy-start(f32[32,32]{0,1:T(8,128)} %copy-done.8) | copy-start | bytes 12292
  1891.8 68.2 %copy-start.11 = (f32[32,32]{0,1:T(8,128)S(1)}, f32[32,32]{0,1:T(8,128)}, u32[]{:S(2)}) copy-start(f32[32,32]{0,1:T(8,128)} %copy-done.10) | copy-start | bytes 12292
  2024.3 280.0 %all-to-all-start.3 = ((f32[3,2,256,4096]{2,1,0,3:T(2,128)}), f32[3,2,256,4096]{2,1,0,3:T(2,128)}, u32[]{:S(2)}, u32[]{:S(2)}) async-start(f32[3,2,256,4096]{2,1,0,3:T(2,128)} %bitcast.106), calls=%async_computation.3 | async-start | bytes 50331648 | tf_op jit(solution)/shard_map/all_to_all | solution.py:101
  2304.3 550.6 %all-to-all-start.1 = ((f32[3,2,4096,256]{3,1,0,2:T(2,128)}), f32[3,2,4096,256]{3,1,0,2:T(2,128)}, u32[]{:S(2)}, u32[]{:S(2)}) async-start(f32[3,2,4096,256]{3,1,0,2:T(2,128)} %bitcast.105), calls=%async_computation.1 | async-start | bytes 50331648 | tf_op jit(solution)/shard_map/all_to_all | solution.py:97
  2357.2 19.5 collective-permute-start
  2357.2 37.5 %collective-permute-start.1 = (f32[3,1,1024,1024]{2,3,1,0:T(8,128)}, f32[3,1,1024,1024]{2,3,1,0:T(8,128)}, u32[]{:S(2)}, u32[]{:S(2)}) collective-permute-start(f32[3,1,1024,1024]{2,3,1,0:T(8,128)} %get-tuple-element.35), channel_id=1, source_target_pairs={{0,16},{16,0},{1,17},{17,1},{2,18},{18,2},{3,19},{19,3},{4,20},{20... | collective-permute-start | bytes 37748744 | tf_op jit(solution)/shard_map/ppermute | solution.py:24
  2976.1 28.2 copy-start.18
  2976.1 28.2 copy-start.19
where the time goes:
time: 3060 us; the launch traced here: 3040 us
  waiting for transfers between devices  1460 us (48%)
  local copies, waits for them, and re-layouts  601 us (20%)
  other arithmetic  479 us (16%)
  matrix products  425 us (14%)
  blocking collectives  41.3 us (1%)
  starting transfers between devices  37.3 us (1%)
    all_to_all x1, waiting for transfers between devices, per_device(): lax.all_to_all(velocity, 'row', split_axis=3, concat_axis=2, tiled=True)  612 us
    all_to_all x1, waiting for transfers between devices, per_device(): lax.all_to_all(velocity, 'col', split_axis=2, concat_axis=3, tiled=True)  327 us
    all_to_all x1, waiting for transfers between devices, along_rows(): lax.all_to_all(back_turned, 'row', split_axis=2, concat_axis=3, tiled=True)  278 us
    dot_general x4, matrix products, right_mult(): return jnp.einsum('...kn,nm->...km', values, coeffs, precision=precise)  264 us
    all_to_all x1, waiting for transfers between devices, along_cols(): lax.all_to_all(derivative_last(pencil), 'col', split_axis=3, concat_axis=...  207 us
    dot_general x4, matrix products, left_mult(): return jnp.einsum('kn,...nm->...km', coeffs, values, precision=precise)  160 us
    unnamed x46, local copies, waits for them, and re-layouts  117 us
    concatenate x2, local copies, waits for them, and re-layouts, derivative_last(): jnp.concatenate([-wavenum * section_c[..., second:], wavenum * section_c[...  99.4 us
  transfers between devices with their start and end apart: 6, of which 6 were waited for; matrix products, arithmetic and copies ran while one was open for 14% of the time, Pallas kernels for 0%

commit v1 on v0

v1 whole, which is shorter than its diff:
```python
import math

import jax
import jax.numpy as jnp
from jax import lax
from jax.sharding import PartitionSpec as P

N = 4096
FINE = 32
COARSE = 1024
SPLITS = 2


precise = lax.Precision.HIGH


def with_halo(cells, sides, width):
    for axis, dim in sides:
        count = lax.axis_size(axis)
        head = lax.slice_in_dim(cells, 0, width, axis=dim)
        tail = lax.slice_in_dim(cells, cells.shape[dim] - width, cells.shape[dim], axis=dim)
        cells = jnp.concatenate(
            [
                lax.ppermute(tail, axis, [(i, (i + 1) % count) for i in range(count)]),
                cells,
                lax.ppermute(head, axis, [((i + 1) % count, i) for i in range(count)]),
            ],
            axis=dim,
        )
    return cells


def kernel_table(size, skew):
    i = lax.broadcasted_iota(jnp.int32, (size, size), 0)
    j = lax.broadcasted_iota(jnp.int32, (size, size), 1)
    shift = i - j
    sign = jnp.where(shift % 2 == 0, 1.0, -1.0)
    wrapped = jnp.where(shift > size // 2, shift - size, shift)
    wrapped = jnp.where(shift < -(size // 2), shift + size, wrapped)
    angle = wrapped.astype(jnp.float32) * (math.pi / size)
    safe = jnp.where(shift == 0, 1.0, angle)
    if skew:
        top = jnp.where(wrapped == shift, 1.0, -1.0)
    else:
        top = jnp.where(jnp.abs(shift) * 2 == size, 0.0, jnp.cos(safe))
    value = sign * (math.pi / size) * top / jnp.sin(safe)
    return jnp.where(shift == 0, 0.0, value)


def make_tables(length):
    tables = []
    size = length
    for _ in range(SPLITS):
        size //= 2
        tables.append(kernel_table(size, True))
    tables.append(kernel_table(size, False))
    return tables


def apply_table(table, values, dim):
    if dim == 1:
        return jnp.einsum("ij,zjm->zim", table, values, precision=precise)
    return jnp.einsum("zmj,ij->zmi", values, table, precision=precise)


def split_derivative(values, tables, dim, scale):
    if len(tables) == 1:
        return apply_table(tables[0], values, dim) * scale
    half = values.shape[dim] // 2
    low = lax.slice_in_dim(values, 0, half, axis=dim)
    high = lax.slice_in_dim(values, half, 2 * half, axis=dim)
    even = split_derivative(low + high, tables[1:], dim, scale * 0.5)
    odd = apply_table(tables[0], low - high, dim) * (scale * 0.5)
    return jnp.concatenate([even + odd, even - odd], axis=dim)


def take(values, index, size, dim):
    return lax.dynamic_slice_in_dim(values, index * size, size, axis=dim)


def send_out(field, axis, dim):
    count = lax.axis_size(axis)
    me = lax.axis_index(axis)
    other = 3 - dim
    size = field.shape[other] // count
    pieces = [None] * count
    pieces[0] = take(field, me, size, other)
    for step in (range(1, count)):
        block = take(field, (me + step) % count, size, other)
        moved = lax.ppermute(block, axis, [(i, (i + step) % count) for i in range(count)])
        pieces[count - step] = moved
    return jnp.concatenate(pieces, axis=dim)


def send_back(line, axis, dim):
    count = lax.axis_size(axis)
    me = lax.axis_index(axis)
    other = 3 - dim
    length = line.shape[dim] // count
    size = line.shape[other]
    shape = list(line.shape)
    shape[dim] = length
    shape[other] = size * count
    result = jnp.zeros(shape, line.dtype)
    for step in range(count):
        block = lax.slice_in_dim(line, step * length, (step + 1) * length, axis=dim)
        if step:
            block = lax.ppermute(block, axis, [(i, (i + step) % count) for i in range(count)])
        source = (me - step + count) % count
        result = lax.dynamic_update_slice_in_dim(result, block, source * size, axis=other)
    return result


def per_device(velocity):
    x_local = velocity.shape[2]
    y_local = velocity.shape[3]
    plane_count = velocity.shape[1] * lax.axis_size("plane")
    rows = lax.axis_size("row")
    cols = lax.axis_size("col")
    x_lines = [send_out(velocity[c], "row", 1) for c in range(3)]
    y_lines = [send_out(velocity[c], "col", 2) for c in range(3)]
    x_tables = make_tables(x_local * rows)
    y_tables = x_tables if x_local * rows == y_local * cols else make_tables(y_local * cols)
    grad_x = [send_back(split_derivative(x_lines[c], x_tables, 1, 1.0), "row", 1) for c in range(3)]
    grad_y = [send_back(split_derivative(y_lines[c], y_tables, 2, 1.0), "col", 2) for c in range(3)]
    padded = with_halo(velocity, (("plane", 1),), 1)
    grad_z = (padded[:, 2:] - padded[:, :-2]) * 0.5
    cross_xy = grad_y[0] + grad_x[1]
    cross_xz = grad_z[0] + grad_x[2]
    cross_yz = grad_z[1] + grad_y[2]
    dissip = grad_x[0] * grad_x[0] + grad_y[1] * grad_y[1] + grad_z[2] * grad_z[2]
    dissip = dissip + 0.5 * (cross_xy * cross_xy + cross_xz * cross_xz + cross_yz * cross_yz)
    column_sum = jnp.sum(dissip, axis=0)
    fine_local = column_sum.reshape(x_local // FINE, FINE, y_local // FINE, FINE).sum(axis=(1, 3))
    fine_total = lax.psum(fine_local, "plane")
    fine_means = fine_total * (1.0 / (plane_count * FINE * FINE))
    local_total = jnp.sum(fine_local)
    row_boxes = x_local * rows // COARSE
    col_boxes = y_local * cols // COARSE
    box_row = lax.axis_index("row") * x_local // COARSE
    box_col = lax.axis_index("col") * y_local // COARSE
    rows_hit = (lax.iota(jnp.int32, row_boxes) == box_row).astype(jnp.float32)
    cols_hit = (lax.iota(jnp.int32, col_boxes) == box_col).astype(jnp.float32)
    partial_map = rows_hit[:, None] * cols_hit[None, :] * local_total
    coarse_total = lax.psum(partial_map, ("plane", "row", "col"))
    coarse_means = coarse_total * (1.0 / (plane_count * COARSE * COARSE))
    return (dissip, fine_means, coarse_means)


def solution(mesh):
    in_specs = (P(None, "plane", "row", "col"),)
    out_specs = (P("plane", "row", "col"), P("row", "col"), P())
    return jax.shard_map(
        per_device, mesh=mesh, in_specs=in_specs, out_specs=out_specs, check_vma=False
    )
```

time: 3060 us -> 1950 us (0.64)
  waiting for transfers between devices: 1460 us -> 588 us
  other arithmetic: 479 us -> 79 us
  matrix products: 425 us -> 820 us
  local copies, waits for them, and re-layouts: 601 us -> 232 us
  starting transfers between devices: 37.3 us -> 174 us
    all_to_all x4 -> x0, waiting for transfers between devices: 1420 us -> none  [the longest x1 612 us: per_device(): lax.all_to_all(velocity, 'row', split_axis=3, concat_axis=2, tiled=True)]
    ppermute x0 -> x36, waiting for transfers between devices: none -> 588 us  [the longest x18 400 us: send_back(): lax.ppermute(block, axis, [(i, (i + step) % count) for i in range(count)])]
    dot_general x8 -> x18, matrix products: 425 us -> 820 us  [the longest x9 437 us: apply_table(): return jnp.einsum('ij,zjm->zim', table, values, precision=precise)]
    ppermute x0 -> x36, starting transfers between devices: none -> 173 us  [the longest x18 152 us: send_back(): lax.ppermute(block, axis, [(i, (i + step) % count) for i in range(count)])]
    all_to_all x5 -> x0, local copies, waits for them, and re-layouts: 150 us -> none  [the longest x2 62.3 us: per_device(): lax.all_to_all(velocity, 'row', split_axis=3, concat_axis=2, tiled=True)]
    concatenate x4 -> x0, other arithmetic: 138 us -> none  [the longest x2 69 us: derivative_last(): jnp.concatenate([real_b, imag_b], axis=-1)]
    concatenate x2 -> x6, local copies, waits for them, and re-layouts: 99.4 us -> 7.49 us  [send_out(): return jnp.concatenate(pieces, axis=dim)]
    unnamed x46 -> x192, local copies, waits for them, and re-layouts: 117 us -> 27.7 us
  transfers between devices with their start and end apart: 6 -> 38, of which waited for: 6 -> 14; matrix products, arithmetic and copies ran while one was open for 14% -> 52% of each run, Pallas kernels for 0% -> 0%
where the time goes in v1:
time: 1950 us; the launch traced here: 1940 us
  matrix products  820 us (42%)
  waiting for transfers between devices  588 us (30%)
  local copies, waits for them, and re-layouts  232 us (12%)
  starting transfers between devices  174 us (9%)
  other arithmetic  79 us (4%)
  blocking collectives  43.4 us (2%)
    dot_general x9, matrix products, apply_table(): return jnp.einsum('ij,zjm->zim', table, values, precision=precise)  437 us
    ppermute x18, waiting for transfers between devices, send_back(): lax.ppermute(block, axis, [(i, (i + step) % count) for i in range(count)])  400 us
    dot_general x9, matrix products, apply_table(): return jnp.einsum('zmj,ij->zmi', values, table, precision=precise)  383 us
    ppermute x18, waiting for transfers between devices, send_out(): lax.ppermute(block, axis, [(i, (i + step) % count) for i in range(count)])  189 us
    ppermute x18, starting transfers between devices, send_back(): lax.ppermute(block, axis, [(i, (i + step) % count) for i in range(count)])  152 us
    dynamic_update_slice x21, local copies, waits for them, and re-layouts, send_back(): lax.dynamic_update_slice_in_dim(result, block, source * size, axis=other)  41.4 us
    psum x1, blocking collectives, per_device(): coarse_total = lax.psum(partial_map, ('plane', 'row', 'col'))  40.1 us
  transfers between devices with their start and end apart: 38, of which 14 were waited for; matrix products, arithmetic and copies ran while one was open for 52% of the time, Pallas kernels for 0%

profile of v1, /device:TPU:0, one launch (start us, length us, event | category | flops | bytes accessed | tf_op | source)
XLA Modules:
  0.0 1938.6 jit_solution(11708996223326801009)
XLA Ops:
  0.7 18.0 fusion.319
  18.7 7.5 dynamic-slice_bitcast_fusion.3
  32.0 6.6 dynamic-slice_bitcast_fusion.7
  42.8 7.1 dynamic-slice_bitcast_fusion.11
  54.0 6.9 dynamic-slice_bitcast_fusion.15
  60.9 7.1 dynamic-slice_bitcast_fusion.23
  68.0 19.4 %fusion.320 = (f32[3,1,1024,1024]{3,2,1,0:T(8,128)}, f32[3,1,1024,1024]{3,2,1,0:T(8,128)}) fusion(f32[3,2,1024,1024]{3,2,1,0:T(8,128)} %param.1), kind=kLoop, calls=%fused_computation.441 | loop fusion | bytes 50331648 | tf_op jit(solution)/shard_map/slice | solution.py:20
  87.4 32.6 %collective-permute-done.33 = f32[2,256,1024]{2,1,0:T(8,128)} collective-permute-done((f32[2,256,1024]{2,1,0:T(8,128)}, f32[2,256,1024]{2,1,0:T(8,128)}, u32[]{:S(2)}, u32[]{:S(2)}) %collective-permute-start.33) | collective-permute-done | bytes 2097184 | tf_op jit(solution)/shard_map/ppermute | solution.py:90
  120.0 3.8 collective-permute-start.26
  132.1 22.0 %fusion.47 = f32[2,256,1024]{2,1,0:T(8,128)} fusion(f32[2,256,2048]{2,1,0:T(8,128)S(1)} %fusion.71), kind=kOutput, calls=%fused_computation.80 | convolution fusion | flops 3255304192 | bytes 6291456 | tf_op jit(solution)/shard_map/zmj,ij->zmi/dot_general | solution.py:63
  156.7 22.0 %multiply_add_fusion.3 = (f32[2,256,1024]{2,1,0:T(8,128)S(1)}, f32[2,256,1024]{2,1,0:T(8,128)S(1)}) fusion(f32[2,256,1024]{2,1,0:T(8,128)} %fusion.47, f32[2,256,2048]{2,1,0:T(8,128)S(1)} %fusion.71), kind=kOutput, calls=%fused_computation.192 | convolution fusion | flops 3255304192 | bytes 10485760 | tf_op jit(solution)/shard_map/zmj,ij->zmi/dot_general | solution.py:63
  178.9 38.1 %collective-permute-done.15 = f32[2,256,1024]{2,1,0:T(8,128)} collective-permute-done((f32[2,256,1024]{2,1,0:T(8,128)S(1)}, f32[2,256,1024]{2,1,0:T(8,128)}, u32[]{:S(2)}, u32[]{:S(2)}) %collective-permute-start.15) | collective-permute-done | bytes 2097184 | tf_op jit(solution)/shard_map/ppermute | solution.py:90
  217.0 85.7 %multiply_subtract_fusion = (f32[2,256,2048]{2,1,0:T(8,128)}, f32[2,256,2048]{2,1,0:T(8,128)}) fusion(f32[2,256,1024]{2,1,0:T(8,128)S(1)} %get-tuple-element.82, f32[2,256,1024]{2,1,0:T(8,128)S(1)} %get-tuple-element.81, f32[2,256,2048]{2,1,0:T(8,128)S(1)} %fusion.59.clone.5), kind=kOutput, calls=%fused_computation.109 | convolution fusion | flops 13014925312 | bytes 16777216 | tf_op jit(solution)/shard_map/zmj,ij->zmi/dot_general | solution.py:63
  306.3 49.7 %collective-permute-done.21 = f32[2,1024,256]{2,1,0:T(8,128)S(1)} collective-permute-done((f32[2,1024,256]{2,1,0:T(8,128)S(1)}, f32[2,1024,256]{2,1,0:T(8,128)S(1)}, u32[]{:S(2)}, u32[]{:S(2)}) %collective-permute-start.21) | collective-permute-done | bytes 2097184 | tf_op jit(solution)/shard_map/ppermute | solution.py:90
  365.9 26.6 %fusion.49 = f32[2,256,1024]{2,1,0:T(8,128)} fusion(f32[2,2048,256]{2,1,0:T(8,128)S(1)} %fusion.72), kind=kOutput, calls=%fused_computation.82 | convolution fusion | flops 3255304192 | bytes 6291456 | tf_op jit(solution)/shard_map/ij,zjm->zim/dot_general | solution.py:62
  392.6 12.2 collective-permute-done.14
  406.3 21.8 %fusion.53 = f32[2,256,1024]{2,1,0:T(8,128)} fusion(f32[2,256,2048]{2,1,0:T(8,128)S(1)} %fusion.74), kind=kOutput, calls=%fused_computation.86 | convolution fusion | flops 3255304192 | bytes 6291456 | tf_op jit(solution)/shard_map/zmj,ij->zmi/dot_general | solution.py:63
  429.5 26.2 %fusion.51 = f32[2,256,1024]{2,1,0:T(8,128)} fusion(f32[2,2048,256]{2,1,0:T(8,128)S(1)} %fusion.73), kind=kOutput, calls=%fused_computation.84 | convolution fusion | flops 3255304192 | bytes 6291456 | tf_op jit(solution)/shard_map/ij,zjm->zim/dot_general | solution.py:62
  455.7 25.3 %add_bitcast_fusion = (f32[2,1024,256]{1,2,0:T(8,128)S(1)}, f32[2,1024,256]{1,2,0:T(8,128)}) fusion(f32[2,256,1024]{2,1,0:T(8,128)S(1)} %copy-done.80, f32[2,2048,256]{2,1,0:T(8,128)S(1)} %copy-done.42), kind=kOutput, calls=%fused_computation.132 | convolution fusion | flops 3255304192 | bytes 10485760 | tf_op jit(solution)/shard_map/ij,zjm->zim/dot_general | solution.py:62
  481.0 56.0 %collective-permute-done.1 = f32[2,1024,256]{2,1,0:T(8,128)} collective-permute-done((f32[2,1024,256]{2,1,0:T(8,128)S(1)}, f32[2,1024,256]{2,1,0:T(8,128)}, u32[]{:S(2)}, u32[]{:S(2)}) %collective-permute-start.1) | collective-permute-done | bytes 2097184 | tf_op jit(solution)/shard_map/ppermute | solution.py:90
  542.9 20.3 %multiply_add_fusion.4 = (f32[2,256,1024]{2,1,0:T(8,128)S(1)}, f32[2,256,1024]{2,1,0:T(8,128)}) fusion(f32[2,256,1024]{2,1,0:T(8,128)S(1)} %copy-done.79, f32[2,256,2048]{2,1,0:T(8,128)S(1)} %fusion.74), kind=kOutput, calls=%fused_computation.194 | convolution fusion | flops 3255304192 | bytes 10485760 | tf_op jit(solution)/shard_map/zmj,ij->zmi/dot_general | solution.py:63
  568.5 25.4 %add_bitcast_fusion.1 = (f32[2,1024,256]{1,2,0:T(8,128)}, f32[2,1024,256]{1,2,0:T(8,128)}) fusion(f32[2,256,1024]{2,1,0:T(8,128)S(1)} %copy-done.76, f32[2,2048,256]{2,1,0:T(8,128)S(1)} %fusion.73), kind=kOutput, calls=%fused_computation.140 | convolution fusion | flops 3255304192 | bytes 10485760 | tf_op jit(solution)/shard_map/ij,zjm->zim/dot_general | solution.py:62
  596.2 26.6 %fusion.57 = f32[2,256,1024]{2,1,0:T(8,128)S(1)} fusion(f32[2,2048,256]{2,1,0:T(8,128)S(1)} %fusion.76), kind=kOutput, calls=%fused_computation.90 | convolution fusion | flops 3255304192 | bytes 6291456 | tf_op jit(solution)/shard_map/ij,zjm->zim/dot_general | solution.py:62
  622.9 25.5 %add_bitcast_fusion.2 = (f32[2,1024,256]{1,2,0:T(8,128)}, f32[2,1024,256]{1,2,0:T(8,128)}) fusion(f32[2,256,1024]{2,1,0:T(8,128)S(1)} %fusion.57, f32[2,2048,256]{2,1,0:T(8,128)S(1)} %fusion.76), kind=kOutput, calls=%fused_computation.160 | convolution fusion | flops 3255304192 | bytes 10485760 | tf_op jit(solution)/shard_map/ij,zjm->zim/dot_general | solution.py:62
  650.0 94.0 %bitcast_subtract_fusion = (f32[2,2048,256]{1,2,0:T(8,128)}, f32[2,2048,256]{1,2,0:T(8,128)}) fusion(f32[2,1024,256]{1,2,0:T(8,128)S(1)} %copy-done.72, f32[2,1024,256]{1,2,0:T(8,128)S(1)} %get-tuple-element.75, f32[2,2048,256]{2,1,0:T(8,128)S(1)} %fusion.60.clone.5), kind=kOutput, calls=%fused_computation.62 | convolution fusion | flops 13014925312 | bytes 16777216 | tf_op jit(solution)/shard_map/ij,zjm->zim/dot_general | solution.py:62
  745.6 85.9 %multiply_subtract_fusion.1 = (f32[2,256,2048]{2,1,0:T(8,128)}, f32[2,256,2048]{2,1,0:T(8,128)}) fusion(f32[2,256,1024]{2,1,0:T(8,128)S(1)} %copy-done.73, f32[2,256,1024]{2,1,0:T(8,128)S(1)} %get-tuple-element.69, f32[2,256,2048]{2,1,0:T(8,128)S(1)} %fusion.62.clone.2), kind=kOutput, calls=%fused_computation.111 | convolution fusion | flops 13014925312 | bytes 16777216 | tf_op jit(solution)/shard_map/zmj,ij->zmi/dot_general | solution.py:63
  833.8 94.2 %bitcast_subtract_fusion.1 = (f32[2,2048,256]{1,2,0:T(8,128)}, f32[2,2048,256]{1,2,0:T(8,128)}) fusion(f32[2,1024,256]{1,2,0:T(8,128)S(1)} %copy-done.75, f32[2,1024,256]{1,2,0:T(8,128)S(1)} %copy-done.74, f32[2,2048,256]{2,1,0:T(8,128)S(1)} %fusion.61.clone.2), kind=kOutput, calls=%fused_computation.64 | convolution fusion | flops 13014925312 | bytes 16777216 | tf_op jit(solution)/shard_map/ij,zjm->zim/dot_general | solution.py:62
  930.2 92.9 %bitcast_subtract_fusion.2 = (f32[2,2048,256]{1,2,0:T(8,128)S(1)}, f32[2,2048,256]{1,2,0:T(8,128)S(1)}) fusion(f32[2,1024,256]{1,2,0:T(8,128)S(1)} %copy-done.78, f32[2,1024,256]{1,2,0:T(8,128)S(1)} %copy-done.77, f32[2,2048,256]{2,1,0:T(8,128)S(1)} %fusion.64.clone.2), kind=kOutput, calls=%fused_computation.66 | convolution fusion | flops 13014925312 | bytes 16777216 | tf_op jit(solution)/shard_map/ij,zjm->zim/dot_general | solution.py:62
  1050.9 19.6 %collective-permute-done.37 = f32[2,256,1024]{2,1,0:T(8,128)} collective-permute-done((f32[2,256,1024]{2,1,0:T(8,128)}, f32[2,256,1024]{2,1,0:T(8,128)}, u32[]{:S(2)}, u32[]{:S(2)}) %collective-permute-start.37) | collective-permute-done | bytes 2097184 | tf_op jit(solution)/shard_map/ppermute | solution.py:108
  1070.5 12.2 collective-permute-done.29
  1085.2 20.4 %fusion.55 = f32[2,256,1024]{2,1,0:T(8,128)S(1)} fusion(f32[2,256,2048]{2,1,0:T(8,128)S(1)} %fusion.75), kind=kOutput, calls=%fused_computation.88 | convolution fusion | flops 3255304192 | bytes 6291456 | tf_op jit(solution)/shard_map/zmj,ij->zmi/dot_general | solution.py:63
  1105.6 67.0 %collective-permute-done.30 = f32[2,1024,256]{1,2,0:T(8,128)} collective-permute-done((f32[2,1024,256]{1,2,0:T(8,128)}, f32[2,1024,256]{1,2,0:T(8,128)}, u32[]{:S(2)}, u32[]{:S(2)}) %collective-permute-start.30) | collective-permute-done | bytes 2097184 | tf_op jit(solution)/shard_map/ppermute | solution.py:108
  1173.2 44.3 %collective-permute-done.23 = f32[2,1024,256]{1,2,0:T(8,128)S(1)} collective-permute-done((f32[2,1024,256]{1,2,0:T(8,128)}, f32[2,1024,256]{1,2,0:T(8,128)S(1)}, u32[]{:S(2)}, u32[]{:S(2)}) %collective-permute-start.23) | collective-permute-done | bytes 2097184 | tf_op jit(solution)/shard_map/ppermute | solution.py:108
  1217.5 132.5 %collective-permute-start.3 = (f32[2,1024,256]{1,2,0:T(8,128)S(1)}, f32[2,1024,256]{1,2,0:T(8,128)S(1)}, u32[]{:S(2)}, u32[]{:S(2)}) collective-permute-start(f32[2,1024,256]{1,2,0:T(8,128)S(1)} %get-tuple-element.49), channel_id=1, source_target_pairs={{0,4},{4,8},{8,12},{12,0},{1,5},{5,9},{9,13},{13,1},{2,6},{6,10},{... | collective-permute-start | bytes 6291464 | tf_op jit(solution)/shard_map/ppermute | solution.py:108
  1350.0 46.3 %collective-permute-done.24 = f32[2,1024,256]{1,2,0:T(8,128)S(1)} collective-permute-done((f32[2,1024,256]{1,2,0:T(8,128)}, f32[2,1024,256]{1,2,0:T(8,128)S(1)}, u32[]{:S(2)}, u32[]{:S(2)}) %collective-permute-start.24) | collective-permute-done | bytes 2097184 | tf_op jit(solution)/shard_map/ppermute | solution.py:108
  1404.6 19.2 multiply_add_fusion.5
  1424.7 106.5 %collective-permute-done.4 = f32[2,1024,256]{1,2,0:T(8,128)S(1)} collective-permute-done((f32[2,1024,256]{1,2,0:T(8,128)S(1)}, f32[2,1024,256]{1,2,0:T(8,128)S(1)}, u32[]{:S(2)}, u32[]{:S(2)}) %collective-permute-start.4) | collective-permute-done | bytes 2097184 | tf_op jit(solution)/shard_map/ppermute | solution.py:108
  1532.2 43.8 %collective-permute-done.5 = f32[2,1024,256]{1,2,0:T(8,128)S(1)} collective-permute-done((f32[2,1024,256]{1,2,0:T(8,128)S(1)}, f32[2,1024,256]{1,2,0:T(8,128)S(1)}, u32[]{:S(2)}, u32[]{:S(2)}) %collective-permute-start.5) | collective-permute-done | bytes 2097184 | tf_op jit(solution)/shard_map/ppermute | solution.py:108
  1577.1 85.7 %multiply_subtract_fusion.2 = (f32[2,256,2048]{2,1,0:T(8,128)}, f32[2,256,2048]{2,1,0:T(8,128)}) fusion(f32[2,256,1024]{2,1,0:T(8,128)S(1)} %get-tuple-element.58, f32[2,256,1024]{2,1,0:T(8,128)S(1)} %get-tuple-element.57, f32[2,256,2048]{2,1,0:T(8,128)S(1)} %fusion.63.clone.2), kind=kOutput, calls=%fused_computation.113 | convolution fusion | flops 13014925312 | bytes 16777216 | tf_op jit(solution)/shard_map/zmj,ij->zmi/dot_general | solution.py:63
  1675.6 4.8 broadcast.88.clone.5
  1686.6 4.4 broadcast.88.clone.4
  1752.6 17.7 collective-permute-done.9
  1771.8 42.4 %collective-permute-done.10 = f32[2,256,1024]{2,1,0:T(8,128)} collective-permute-done((f32[2,256,1024]{2,1,0:T(8,128)}, f32[2,256,1024]{2,1,0:T(8,128)}, u32[]{:S(2)}, u32[]{:S(2)}) %collective-permute-start.10) | collective-permute-done | bytes 2097184 | tf_op jit(solution)/shard_map/ppermute | solution.py:108
  1820.8 20.5 %fusion.1 = f32[3,2,1024,1024]{3,2,1,0:T(8,128)} fusion(f32[3,2,1024,1024]{3,2,1,0:T(8,128)S(1)} %bitcast.178, f32[3,1,1024,1024]{3,2,1,0:T(8,128)} %collective-permute-done.13, f32[3,1,1024,1024]{3,2,1,0:T(8,128)} %collective-permute-done.12), kind=kLoop, calls=%fused_computation.3 | loop fusion | flops 25165824 | bytes 75497472 | tf_op jit(solution)/shard_map/mul | solution.py:127
  1841.3 32.5 %fusion.317 = (f32[]{:T(128)}, f32[1024,1024]{1,0:T(8,128)}, f32[2,1024,1024]{2,1,0:T(8,128)}) fusion(f32[2,1024,1024]{2,1,0:T(8,128)} %copy-done.1, f32[3,2,1024,1024]{3,2,1,0:T(8,128)} %fusion.1, f32[2,1024,1024]{2,1,0:T(8,128)} %constant_dynamic-update-slice_fusion.15, f32[2,1024,1024]{2,1,0:T(8,128)} %copy-done.3, ...), kind=kLoop, calls=%fused_computation.439 | loop fusion | flops 34603008 | bytes 88080384 | tf_op jit(solution)/shard_map/reduce_sum | solution.py:137
  1873.8 11.7 reshape.44
  1885.5 7.3 reduce_sum.28
  1897.5 40.1 %psum.15 = f32[4,4]{1,0:T(4,128)S(1)} all-reduce(f32[4,4]{1,0:T(4,128)S(1)} %multiply_multiply_fusion), channel_id=1, replica_groups=mesh['plane'=2,'row'=4,'col'=4] {'plane','row','col'}, use_global_device_ids=true, to_apply=%region_4.5 | all-reduce | flops 16 | bytes 128 | tf_op jit(solution)/shard_map/psum | solution.py:145
  (329 shorter events, 198.0 us)
Async XLA Ops:
  26.1 93.9 %collective-permute-start.33 = (f32[2,256,1024]{2,1,0:T(8,128)}, f32[2,256,1024]{2,1,0:T(8,128)}, u32[]{:S(2)}, u32[]{:S(2)}) collective-permute-start(f32[2,256,1024]{2,1,0:T(8,128)} %get-tuple-element.45), channel_id=1, source_target_pairs={{0,2},{1,3},{2,0},{3,1},{4,6},{5,7},{6,4},{7,5},{8,10},{9,11},{10,... | collective-permute-start | bytes 6291464 | tf_op jit(solution)/shard_map/ppermute | solution.py:90
  29.1 96.6 %collective-permute-start.34 = (f32[2,256,1024]{2,1,0:T(8,128)}, f32[2,256,1024]{2,1,0:T(8,128)}, u32[]{:S(2)}, u32[]{:S(2)}) collective-permute-start(f32[2,256,1024]{2,1,0:T(8,128)} %get-tuple-element.44), channel_id=1, source_target_pairs={{0,1},{1,2},{2,3},{3,0},{4,5},{5,6},{6,7},{7,4},{8,9},{9,10},{10,1... | collective-permute-start | bytes 6291464 | tf_op jit(solution)/shard_map/ppermute | solution.py:90
  30.6 98.5 %collective-permute-start.32 = (f32[2,256,1024]{2,1,0:T(8,128)}, f32[2,256,1024]{2,1,0:T(8,128)}, u32[]{:S(2)}, u32[]{:S(2)}) collective-permute-start(f32[2,256,1024]{2,1,0:T(8,128)} %get-tuple-element.46), channel_id=1, source_target_pairs={{0,3},{1,0},{2,1},{3,2},{4,7},{5,4},{6,5},{7,6},{8,11},{9,8},{10,9... | collective-permute-start | bytes 6291464 | tf_op jit(solution)/shard_map/ppermute | solution.py:90
  38.6 326.7 %copy-start.17 = (f32[2,1024,256]{2,1,0:T(8,128)}, f32[2,1024,256]{2,1,0:T(8,128)S(1)}, u32[]{:S(2)}) copy-start(f32[2,1024,256]{2,1,0:T(8,128)S(1)} %get-tuple-element.37) | copy-start | bytes 6291460
  38.6 140.2 %collective-permute-start.27 = (f32[2,1024,256]{2,1,0:T(8,128)}, f32[2,1024,256]{2,1,0:T(8,128)}, u32[]{:S(2)}, u32[]{:S(2)}) collective-permute-start(f32[2,1024,256]{2,1,0:T(8,128)} %get-tuple-element.39), channel_id=1, source_target_pairs={{0,8},{4,12},{8,0},{12,4},{1,9},{5,13},{9,1},{13,5},{2,10},{6,14},... | collective-permute-start | bytes 6291464 | tf_op jit(solution)/shard_map/ppermute | solution.py:90
  41.2 315.4 %collective-permute-start.28 = (f32[2,1024,256]{2,1,0:T(8,128)}, f32[2,1024,256]{2,1,0:T(8,128)}, u32[]{:S(2)}, u32[]{:S(2)}) collective-permute-start(f32[2,1024,256]{2,1,0:T(8,128)} %get-tuple-element.38), channel_id=1, source_target_pairs={{0,4},{4,8},{8,12},{12,0},{1,5},{5,9},{9,13},{13,1},{2,6},{6,10},{... | collective-permute-start | bytes 6291464 | tf_op jit(solution)/shard_map/ppermute | solution.py:90
  120.0 243.7 %collective-permute-start.26 = (f32[2,1024,256]{2,1,0:T(8,128)S(1)}, f32[2,1024,256]{2,1,0:T(8,128)S(1)}, u32[]{:S(2)}, u32[]{:S(2)}) collective-permute-start(f32[2,1024,256]{2,1,0:T(8,128)S(1)} %copy-done.53), channel_id=1, source_target_pairs={{0,12},{4,0},{8,4},{12,8},{1,13},{5,1},{9,5},{13,9},{2,14},{6,2},{... | collective-permute-start | bytes 6291464 | tf_op jit(solution)/shard_map/ppermute | solution.py:90
  125.7 91.3 %collective-permute-start.15 = (f32[2,256,1024]{2,1,0:T(8,128)S(1)}, f32[2,256,1024]{2,1,0:T(8,128)}, u32[]{:S(2)}, u32[]{:S(2)}) collective-permute-start(f32[2,256,1024]{2,1,0:T(8,128)S(1)} %get-tuple-element.33), channel_id=1, source_target_pairs={{0,2},{1,3},{2,0},{3,1},{4,6},{5,7},{6,4},{7,5},{8,10},{9,11},{10,... | collective-permute-start | bytes 6291464 | tf_op jit(solution)/shard_map/ppermute | solution.py:90
  129.1 229.5 %collective-permute-start.16 = (f32[2,256,1024]{2,1,0:T(8,128)}, f32[2,256,1024]{2,1,0:T(8,128)}, u32[]{:S(2)}, u32[]{:S(2)}) collective-permute-start(f32[2,256,1024]{2,1,0:T(8,128)} %get-tuple-element.32), channel_id=1, source_target_pairs={{0,1},{1,2},{2,3},{3,0},{4,5},{5,6},{6,7},{7,4},{8,9},{9,10},{10,1... | collective-permute-start | bytes 6291464 | tf_op jit(solution)/shard_map/ppermute | solution.py:90
  178.8 177.2 %collective-permute-start.21 = (f32[2,1024,256]{2,1,0:T(8,128)S(1)}, f32[2,1024,256]{2,1,0:T(8,128)S(1)}, u32[]{:S(2)}, u32[]{:S(2)}) collective-permute-start(f32[2,1024,256]{2,1,0:T(8,128)S(1)} %copy-done.55), channel_id=1, source_target_pairs={{0,8},{4,12},{8,0},{12,4},{1,9},{5,13},{9,1},{13,5},{2,10},{6,14},... | collective-permute-start | bytes 6291464 | tf_op jit(solution)/shard_map/ppermute | solution.py:90
  217.0 145.1 %collective-permute-start.22 = (f32[2,1024,256]{2,1,0:T(8,128)S(1)}, f32[2,1024,256]{2,1,0:T(8,128)S(1)}, u32[]{:S(2)}, u32[]{:S(2)}) collective-permute-start(f32[2,1024,256]{2,1,0:T(8,128)S(1)} %copy-done.54), channel_id=1, source_target_pairs={{0,4},{4,8},{8,12},{12,0},{1,5},{5,9},{9,13},{13,1},{2,6},{6,10},{... | collective-permute-start | bytes 6291464 | tf_op jit(solution)/shard_map/ppermute | solution.py:90
  356.0 48.8 %collective-permute-start.14 = (f32[2,256,1024]{2,1,0:T(8,128)}, f32[2,256,1024]{2,1,0:T(8,128)S(1)}, u32[]{:S(2)}, u32[]{:S(2)}) collective-permute-start(f32[2,256,1024]{2,1,0:T(8,128)} %get-tuple-element.34), channel_id=1, source_target_pairs={{0,3},{1,0},{2,1},{3,2},{4,7},{5,4},{6,5},{7,6},{8,11},{9,8},{10,9... | collective-permute-start | bytes 6291464 | tf_op jit(solution)/shard_map/ppermute | solution.py:90
  356.6 71.5 %collective-permute-start.20 = (f32[2,1024,256]{2,1,0:T(8,128)}, f32[2,1024,256]{2,1,0:T(8,128)S(1)}, u32[]{:S(2)}, u32[]{:S(2)}) collective-permute-start(f32[2,1024,256]{2,1,0:T(8,128)} %get-tuple-element.28), channel_id=1, source_target_pairs={{0,12},{4,0},{8,4},{12,8},{1,13},{5,1},{9,5},{13,9},{2,14},{6,2},{... | collective-permute-start | bytes 6291464 | tf_op jit(solution)/shard_map/ppermute | solution.py:90
  358.6 664.4 %collective-permute-start.7 = (f32[2,256,1024]{2,1,0:T(8,128)}, f32[2,256,1024]{2,1,0:T(8,128)}, u32[]{:S(2)}, u32[]{:S(2)}) collective-permute-start(f32[2,256,1024]{2,1,0:T(8,128)} %get-tuple-element.21), channel_id=1, source_target_pairs={{0,2},{1,3},{2,0},{3,1},{4,6},{5,7},{6,4},{7,5},{8,10},{9,11},{10,... | collective-permute-start | bytes 6291464 | tf_op jit(solution)/shard_map/ppermute | solution.py:90
  362.1 669.9 %collective-permute-start.8 = (f32[2,256,1024]{2,1,0:T(8,128)}, f32[2,256,1024]{2,1,0:T(8,128)}, u32[]{:S(2)}, u32[]{:S(2)}) collective-permute-start(f32[2,256,1024]{2,1,0:T(8,128)} %get-tuple-element.20), channel_id=1, source_target_pairs={{0,1},{1,2},{2,3},{3,0},{4,5},{5,6},{6,7},{7,4},{8,9},{9,10},{10,1... | collective-permute-start | bytes 6291464 | tf_op jit(solution)/shard_map/ppermute | solution.py:90
  363.7 678.5 %collective-permute-start.6 = (f32[2,256,1024]{2,1,0:T(8,128)}, f32[2,256,1024]{2,1,0:T(8,128)}, u32[]{:S(2)}, u32[]{:S(2)}) collective-permute-start(f32[2,256,1024]{2,1,0:T(8,128)} %get-tuple-element.22), channel_id=1, source_target_pairs={{0,3},{1,0},{2,1},{3,2},{4,7},{5,4},{6,5},{7,6},{8,11},{9,8},{10,9... | collective-permute-start | bytes 6291464 | tf_op jit(solution)/shard_map/ppermute | solution.py:90
  404.7 132.3 %collective-permute-start.1 = (f32[2,1024,256]{2,1,0:T(8,128)S(1)}, f32[2,1024,256]{2,1,0:T(8,128)}, u32[]{:S(2)}, u32[]{:S(2)}) collective-permute-start(f32[2,1024,256]{2,1,0:T(8,128)S(1)} %copy-done.58), channel_id=1, source_target_pairs={{0,8},{4,12},{8,0},{12,4},{1,9},{5,13},{9,1},{13,5},{2,10},{6,14},... | collective-permute-start | bytes 6291464 | tf_op jit(solution)/shard_map/ppermute | solution.py:90
  428.1 135.1 %collective-permute-start.2 = (f32[2,1024,256]{2,1,0:T(8,128)S(1)}, f32[2,1024,256]{2,1,0:T(8,128)S(1)}, u32[]{:S(2)}, u32[]{:S(2)}) collective-permute-start(f32[2,1024,256]{2,1,0:T(8,128)S(1)} %copy-done.57), channel_id=1, source_target_pairs={{0,4},{4,8},{8,12},{12,0},{1,5},{5,9},{9,13},{13,1},{2,6},{6,10},{... | collective-permute-start | bytes 6291464 | tf_op jit(solution)/shard_map/ppermute | solution.py:90
  537.0 56.8 %collective-permute-start = (f32[2,1024,256]{2,1,0:T(8,128)S(1)}, f32[2,1024,256]{2,1,0:T(8,128)S(1)}, u32[]{:S(2)}, u32[]{:S(2)}) collective-permute-start(f32[2,1024,256]{2,1,0:T(8,128)S(1)} %copy-done.56), channel_id=1, source_target_pairs={{0,12},{4,0},{8,4},{12,8},{1,13},{5,1},{9,5},{13,9},{2,14},{6,2},{... | collective-permute-start | bytes 6291464 | tf_op jit(solution)/shard_map/ppermute | solution.py:90
  563.2 484.3 %collective-permute-start.35 = (f32[2,256,1024]{2,1,0:T(8,128)}, f32[2,256,1024]{2,1,0:T(8,128)}, u32[]{:S(2)}, u32[]{:S(2)}) collective-permute-start(f32[2,256,1024]{2,1,0:T(8,128)} %get-tuple-element.79), channel_id=1, source_target_pairs={{0,1},{1,2},{2,3},{3,0},{4,5},{5,6},{6,7},{7,4},{8,9},{9,10},{10,1... | collective-permute-start | bytes 6291464 | tf_op jit(solution)/shard_map/ppermute | solution.py:108
  593.9 457.0 %collective-permute-start.36 = (f32[2,256,1024]{2,1,0:T(8,128)}, f32[2,256,1024]{2,1,0:T(8,128)}, u32[]{:S(2)}, u32[]{:S(2)}) collective-permute-start(f32[2,256,1024]{2,1,0:T(8,128)} %get-tuple-element.78), channel_id=1, source_target_pairs={{0,2},{1,3},{2,0},{3,1},{4,6},{5,7},{6,4},{7,5},{8,10},{9,11},{10,... | collective-permute-start | bytes 6291464 | tf_op jit(solution)/shard_map/ppermute | solution.py:108
  650.0 94.0 %copy-start.38 = (f32[2,256,1024]{2,1,0:T(8,128)S(1)}, f32[2,256,1024]{2,1,0:T(8,128)}, u32[]{:S(2)}) copy-start(f32[2,256,1024]{2,1,0:T(8,128)} %copy-done.37) | copy-start | bytes 6291460
  833.7 94.2 %copy-start.13 = (f32[2,2048,256]{2,1,0:T(8,128)S(1)}, f32[2,2048,256]{2,1,0:T(8,128)}, u32[]{:S(2)}) copy-start(f32[2,2048,256]{2,1,0:T(8,128)} %copy-done.12) | copy-start | bytes 12582916
  833.7 94.2 %copy-start.21 = (f32[2,1024,256]{2,1,0:T(8,128)S(1)}, f32[2,1024,256]{2,1,0:T(8,128)}, u32[]{:S(2)}) copy-start(f32[2,1024,256]{2,1,0:T(8,128)} %get-tuple-element.13) | copy-start | bytes 6291460
  833.7 94.2 %copy-start.40 = (f32[2,1024,256]{2,1,0:T(8,128)S(1)}, f32[2,1024,256]{2,1,0:T(8,128)}, u32[]{:S(2)}) copy-start(f32[2,1024,256]{2,1,0:T(8,128)} %copy-done.39) | copy-start | bytes 6291460
  1023.1 47.5 %collective-permute-start.37 = (f32[2,256,1024]{2,1,0:T(8,128)}, f32[2,256,1024]{2,1,0:T(8,128)}, u32[]{:S(2)}, u32[]{:S(2)}) collective-permute-start(f32[2,256,1024]{2,1,0:T(8,128)} %get-tuple-element.77), channel_id=1, source_target_pairs={{0,3},{1,0},{2,1},{3,2},{4,7},{5,4},{6,5},{7,6},{8,11},{9,8},{10,9... | collective-permute-start | bytes 6291464 | tf_op jit(solution)/shard_map/ppermute | solution.py:108
  1032.0 50.7 %collective-permute-start.29 = (f32[2,1024,256]{1,2,0:T(8,128)}, f32[2,1024,256]{1,2,0:T(8,128)}, u32[]{:S(2)}, u32[]{:S(2)}) collective-permute-start(f32[2,1024,256]{1,2,0:T(8,128)} %get-tuple-element.73), channel_id=1, source_target_pairs={{0,4},{4,8},{8,12},{12,0},{1,5},{5,9},{9,13},{13,1},{2,6},{6,10},{... | collective-permute-start | bytes 6291464 | tf_op jit(solution)/shard_map/ppermute | solution.py:108
  1042.1 130.5 %collective-permute-start.30 = (f32[2,1024,256]{1,2,0:T(8,128)}, f32[2,1024,256]{1,2,0:T(8,128)}, u32[]{:S(2)}, u32[]{:S(2)}) collective-permute-start(f32[2,1024,256]{1,2,0:T(8,128)} %get-tuple-element.72), channel_id=1, source_target_pairs={{0,8},{4,12},{8,0},{12,4},{1,9},{5,13},{9,1},{13,5},{2,10},{6,14},... | collective-permute-start | bytes 6291464 | tf_op jit(solution)/shard_map/ppermute | solution.py:108
  1047.5 125.2 %collective-permute-start.31 = (f32[2,1024,256]{1,2,0:T(8,128)}, f32[2,1024,256]{1,2,0:T(8,128)S(1)}, u32[]{:S(2)}, u32[]{:S(2)}) collective-permute-start(f32[2,1024,256]{1,2,0:T(8,128)} %get-tuple-element.71), channel_id=1, source_target_pairs={{0,12},{4,0},{8,4},{12,8},{1,13},{5,1},{9,5},{13,9},{2,14},{6,2},{... | collective-permute-start | bytes 6291464 | tf_op jit(solution)/shard_map/ppermute | solution.py:108
  1050.9 166.6 %collective-permute-start.23 = (f32[2,1024,256]{1,2,0:T(8,128)}, f32[2,1024,256]{1,2,0:T(8,128)S(1)}, u32[]{:S(2)}, u32[]{:S(2)}) collective-permute-start(f32[2,1024,256]{1,2,0:T(8,128)} %get-tuple-element.61), channel_id=1, source_target_pairs={{0,4},{4,8},{8,12},{12,0},{1,5},{5,9},{9,13},{13,1},{2,6},{6,10},{... | collective-permute-start | bytes 6291464 | tf_op jit(solution)/shard_map/ppermute | solution.py:108
  1070.5 325.8 %collective-permute-start.24 = (f32[2,1024,256]{1,2,0:T(8,128)}, f32[2,1024,256]{1,2,0:T(8,128)S(1)}, u32[]{:S(2)}, u32[]{:S(2)}) collective-permute-start(f32[2,1024,256]{1,2,0:T(8,128)} %get-tuple-element.60), channel_id=1, source_target_pairs={{0,8},{4,12},{8,0},{12,4},{1,9},{5,13},{9,1},{13,5},{2,10},{6,14},... | collective-permute-start | bytes 6291464 | tf_op jit(solution)/shard_map/ppermute | solution.py:108
  1082.7 313.6 %collective-permute-start.25 = (f32[2,1024,256]{1,2,0:T(8,128)}, f32[2,1024,256]{1,2,0:T(8,128)S(1)}, u32[]{:S(2)}, u32[]{:S(2)}) collective-permute-start(f32[2,1024,256]{1,2,0:T(8,128)} %get-tuple-element.59), channel_id=1, source_target_pairs={{0,12},{4,0},{8,4},{12,8},{1,13},{5,1},{9,5},{13,9},{2,14},{6,2},{... | collective-permute-start | bytes 6291464 | tf_op jit(solution)/shard_map/ppermute | solution.py:108
  1085.2 312.8 %copy-start.44 = (f32[2,256,2048]{2,1,0:T(8,128)S(1)}, f32[2,256,2048]{2,1,0:T(8,128)}, u32[]{:S(2)}) copy-start(f32[2,256,2048]{2,1,0:T(8,128)} %get-tuple-element.29) | copy-start | bytes 12582916
  1172.7 648.0 %collective-permute-start.13 = (f32[3,1,1024,1024]{3,2,1,0:T(8,128)}, f32[3,1,1024,1024]{3,2,1,0:T(8,128)}, u32[]{:S(2)}, u32[]{:S(2)}) collective-permute-start(f32[3,1,1024,1024]{3,2,1,0:T(8,128)} %get-tuple-element.10), channel_id=1, source_target_pairs={{0,16},{16,0},{1,17},{17,1},{2,18},{18,2},{3,19},{19,3},{4,20},{20... | collective-permute-start | bytes 37748744 | tf_op jit(solution)/shard_map/ppermute | solution.py:24
  1172.7 227.8 %copy-start.59 = (f32[2,1024,256]{1,2,0:T(8,128)}, f32[2,1024,256]{1,2,0:T(8,128)S(1)}, u32[]{:S(2)}) copy-start(f32[2,1024,256]{1,2,0:T(8,128)S(1)} %collective-permute-done.31) | copy-start | bytes 6291460
  1172.7 648.0 %collective-permute-start.12 = (f32[3,1,1024,1024]{3,2,1,0:T(8,128)}, f32[3,1,1024,1024]{3,2,1,0:T(8,128)}, u32[]{:S(2)}, u32[]{:S(2)}) collective-permute-start(f32[3,1,1024,1024]{3,2,1,0:T(8,128)} %get-tuple-element.9), channel_id=1, source_target_pairs={{16,0},{0,16},{17,1},{1,17},{18,2},{2,18},{19,3},{3,19},{20,4},{4,... | collective-permute-start | bytes 37748744 | tf_op jit(solution)/shard_map/ppermute | solution.py:26
  1217.5 183.0 %copy-start.61 = (f32[2,1024,256]{1,2,0:T(8,128)}, f32[2,1024,256]{1,2,0:T(8,128)S(1)}, u32[]{:S(2)}) copy-start(f32[2,1024,256]{1,2,0:T(8,128)S(1)} %collective-permute-done.23) | copy-start | bytes 6291460
  1217.5 206.3 %collective-permute-start.3 = (f32[2,1024,256]{1,2,0:T(8,128)S(1)}, f32[2,1024,256]{1,2,0:T(8,128)S(1)}, u32[]{:S(2)}, u32[]{:S(2)}) collective-permute-start(f32[2,1024,256]{1,2,0:T(8,128)S(1)} %get-tuple-element.49), channel_id=1, source_target_pairs={{0,4},{4,8},{8,12},{12,0},{1,5},{5,9},{9,13},{13,1},{2,6},{6,10},{... | collective-permute-start | bytes 6291464 | tf_op jit(solution)/shard_map/ppermute | solution.py:108
  1396.3 134.9 %collective-permute-start.4 = (f32[2,1024,256]{1,2,0:T(8,128)S(1)}, f32[2,1024,256]{1,2,0:T(8,128)S(1)}, u32[]{:S(2)}, u32[]{:S(2)}) collective-permute-start(f32[2,1024,256]{1,2,0:T(8,128)S(1)} %get-tuple-element.48), channel_id=1, source_target_pairs={{0,8},{4,12},{8,0},{12,4},{1,9},{5,13},{9,1},{13,5},{2,10},{6,14},... | collective-permute-start | bytes 6291464 | tf_op jit(solution)/shard_map/ppermute | solution.py:108
  1396.4 179.7 %collective-permute-start.5 = (f32[2,1024,256]{1,2,0:T(8,128)S(1)}, f32[2,1024,256]{1,2,0:T(8,128)S(1)}, u32[]{:S(2)}, u32[]{:S(2)}) collective-permute-start(f32[2,1024,256]{1,2,0:T(8,128)S(1)} %get-tuple-element.47), channel_id=1, source_target_pairs={{0,12},{4,0},{8,4},{12,8},{1,13},{5,1},{9,5},{13,9},{2,14},{6,2},{... | collective-permute-start | bytes 6291464 | tf_op jit(solution)/shard_map/ppermute | solution.py:108
  1423.8 239.0 %copy-start.65 = (f32[2,1024,256]{1,2,0:T(8,128)}, f32[2,1024,256]{1,2,0:T(8,128)S(1)}, u32[]{:S(2)}) copy-start(f32[2,1024,256]{1,2,0:T(8,128)S(1)} %collective-permute-done.3) | copy-start | bytes 6291460
  1423.9 296.9 %collective-permute-start.17 = (f32[2,256,1024]{2,1,0:T(8,128)}, f32[2,256,1024]{2,1,0:T(8,128)}, u32[]{:S(2)}, u32[]{:S(2)}) collective-permute-start(f32[2,256,1024]{2,1,0:T(8,128)} %get-tuple-element.67), channel_id=1, source_target_pairs={{0,1},{1,2},{2,3},{3,0},{4,5},{5,6},{6,7},{7,4},{8,9},{9,10},{10,1... | collective-permute-start | bytes 6291464 | tf_op jit(solution)/shard_map/ppermute | solution.py:108
  1531.2 131.6 %copy-start.67 = (f32[2,1024,256]{1,2,0:T(8,128)}, f32[2,1024,256]{1,2,0:T(8,128)S(1)}, u32[]{:S(2)}) copy-start(f32[2,1024,256]{1,2,0:T(8,128)S(1)} %collective-permute-done.4) | copy-start | bytes 6291460
  1531.2 192.4 %collective-permute-start.18 = (f32[2,256,1024]{2,1,0:T(8,128)}, f32[2,256,1024]{2,1,0:T(8,128)}, u32[]{:S(2)}, u32[]{:S(2)}) collective-permute-start(f32[2,256,1024]{2,1,0:T(8,128)} %get-tuple-element.66), channel_id=1, source_target_pairs={{0,2},{1,3},{2,0},{3,1},{4,6},{5,7},{6,4},{7,5},{8,10},{9,11},{10,... | collective-permute-start | bytes 6291464 | tf_op jit(solution)/shard_map/ppermute | solution.py:108
  1576.0 150.1 %collective-permute-start.19 = (f32[2,256,1024]{2,1,0:T(8,128)}, f32[2,256,1024]{2,1,0:T(8,128)}, u32[]{:S(2)}, u32[]{:S(2)}) collective-permute-start(f32[2,256,1024]{2,1,0:T(8,128)} %get-tuple-element.65), channel_id=1, source_target_pairs={{0,3},{1,0},{2,1},{3,2},{4,7},{5,4},{6,5},{7,6},{8,11},{9,8},{10,9... | collective-permute-start | bytes 6291464 | tf_op jit(solution)/shard_map/ppermute | solution.py:108
  1720.8 49.5 %collective-permute-start.9 = (f32[2,256,1024]{2,1,0:T(8,128)S(1)}, f32[2,256,1024]{2,1,0:T(8,128)S(1)}, u32[]{:S(2)}, u32[]{:S(2)}) collective-permute-start(f32[2,256,1024]{2,1,0:T(8,128)S(1)} %copy-done.69), channel_id=1, source_target_pairs={{0,1},{1,2},{2,3},{3,0},{4,5},{5,6},{6,7},{7,4},{8,9},{9,10},{10,1... | collective-permute-start | bytes 6291464 | tf_op jit(solution)/shard_map/ppermute | solution.py:108
  1723.6 90.6 %collective-permute-start.10 = (f32[2,256,1024]{2,1,0:T(8,128)}, f32[2,256,1024]{2,1,0:T(8,128)}, u32[]{:S(2)}, u32[]{:S(2)}) collective-permute-start(f32[2,256,1024]{2,1,0:T(8,128)} %get-tuple-element.54), channel_id=1, source_target_pairs={{0,2},{1,3},{2,0},{3,1},{4,6},{5,7},{6,4},{7,5},{8,10},{9,11},{10,... | collective-permute-start | bytes 6291464 | tf_op jit(solution)/shard_map/ppermute | solution.py:108
  1726.1 91.3 %collective-permute-start.11 = (f32[2,256,1024]{2,1,0:T(8,128)}, f32[2,256,1024]{2,1,0:T(8,128)}, u32[]{:S(2)}, u32[]{:S(2)}) collective-permute-start(f32[2,256,1024]{2,1,0:T(8,128)} %get-tuple-element.53), channel_id=1, source_target_pairs={{0,3},{1,0},{2,1},{3,2},{4,7},{5,4},{6,5},{7,6},{8,11},{9,8},{10,9... | collective-permute-start | bytes 6291464 | tf_op jit(solution)/shard_map/ppermute | solution.py:108
  (83 other events, 1989.8 us)
